TPU v7x, 32 devices: a whole 2x2x4 slice. The times are simulated.
32 devices in a mesh: grp: 2 (over x), gy: 8 (over z, y), ch: 2 (over core).
Axes of the slice: x: 2, y: 2, z: 4, core: 2. Of those that a mesh axis runs over, the one named last changes fastest.
Arguments:
- inputs: bfloat16 [256, 8, 16, 256], P(None, 'gy', 'grp'), parts along dimension 2, may hold values from -6 to 6
- cotangent: bfloat16 [256, 8, 16, 256], P('ch', 'gy', 'grp'), parts along dimension 2, may hold values from -6 to 6
- weight: bfloat16 [27, 256, 256], P(None, None, 'ch'), may hold values from -0.078125 to 0.078125
Outputs:
- input_grad: bfloat16 [256, 8, 16, 256], P('ch', 'gy', 'grp'), parts along dimension 2
- weight_grad: float32 [54, 256, 256], P('grp', None, 'ch'), parts along dimension 0
There are 2 independent parts, one for each index of `grp`. A program takes and returns all parts, laid end to end along the dimension named above; an argument that names none is the same for every part. Nothing has to cross between parts.
All inputs are finite; a program needn't handle non-finite values.
Results may differ from a plain program's by a relative error of at most 0.0013.
Values may be sent and summed in bfloat16 or wider, within the bound.
A program may use at most 192 MiB of HBM per device.

v0:
```python
import math
import jax
import jax.numpy as jnp
from jax import lax
from jax.sharding import PartitionSpec as P


def padded(block, sides, width):
    for axis, dim in sides:
        count = lax.axis_size(axis)
        forward = [(i, i + 1) for i in range(count - 1)]
        backward = [(target, source) for source, target in forward]
        low = lax.ppermute(
            lax.slice_in_dim(block, block.shape[dim] - width, None, axis=dim), axis, forward
        )
        high = lax.ppermute(lax.slice_in_dim(block, 0, width, axis=dim), axis, backward)
        block = jnp.concatenate([low, block, high], axis=dim)
    return block


def shift_cells(flat, z_step, x_step, x_count):
    offset = z_step * x_count + x_step
    length = flat.shape[-1]
    if offset > 0:
        filler = jnp.zeros(flat.shape[:-1] + (offset,), flat.dtype)
        moved = jnp.concatenate([filler, flat[..., : length - offset]], axis=-1)
    elif offset < 0:
        filler = jnp.zeros(flat.shape[:-1] + (-offset,), flat.dtype)
        moved = jnp.concatenate([flat[..., -offset:], filler], axis=-1)
    else:
        moved = flat
    if x_step == 0:
        return moved
    column = jnp.arange(length) % x_count - x_step
    keep = (column >= 0) & (column < x_count)
    return jnp.where(keep, moved, jnp.zeros((), flat.dtype))


def grad_group(planes, y_off, x_count):
    row_count = planes.shape[1] - 2
    flat = planes.reshape(planes.shape[0], planes.shape[1], -1)
    window = flat[:, 2 - y_off : 2 - y_off + row_count, :]
    pieces_list = []
    for z_off in range(3):
        for x_off in range(3):
            pieces_list.append(shift_cells(window, z_off - 1, x_off - 1, x_count))
    stacked = jnp.stack(pieces_list, 0)
    return stacked.reshape(9 * planes.shape[0], -1)


def local(inputs, cotangent, weight):
    channel_count = inputs.shape[0]
    local_out = cotangent.shape[0]
    row_count = inputs.shape[1]
    z_count = inputs.shape[2]
    x_count = inputs.shape[3]
    cell_count = row_count * z_count * x_count
    owned_rows = channel_count // lax.axis_size("ch")
    weight_rows = jnp.transpose(weight, (1, 0, 2))
    planes = padded(cotangent, (("gy", 1),), 1)
    stacks = []
    stacks = [grad_group(planes, y_off, x_count) for y_off in range(3)]
    summed = jnp.zeros((owned_rows * lax.axis_size("ch"), cell_count), jnp.float32)
    for partial_y_off in range(3):
        tap_cols = weight_rows[:, 9 * partial_y_off : 9 * partial_y_off + 9, :].reshape(
            owned_rows * lax.axis_size("ch"), -1
        )
        summed = summed + jnp.dot(
            tap_cols, stacks[partial_y_off], preferred_element_type=jnp.float32
        )
    grad_rows = lax.psum_scatter(summed, "ch", scatter_dimension=0, tiled=True)
    input_grad = grad_rows.astype(jnp.bfloat16).reshape(owned_rows, row_count, z_count, x_count)
    tap_grads = []
    input_halo = padded(inputs, (("gy", 1),), 1)
    halo_flat = input_halo.reshape(channel_count, row_count + 2, -1)
    grad_flat = cotangent.reshape(local_out, -1)
    for y_off in range(3):
        window = halo_flat[:, y_off : y_off + row_count, :]
        for z_off in range(3):
            for x_off in range(3):
                moved = shift_cells(window, 1 - z_off, 1 - x_off, x_count).reshape(
                    channel_count, -1
                )
                tap_grads.append(
                    lax.dot_general(
                        moved,
                        grad_flat,
                        (((1,), (1,)), ((), ())),
                        preferred_element_type=jnp.float32,
                    )
                )
    local_grad = jnp.stack(tap_grads, 0)
    norm_factor = 1.0 / math.sqrt(row_count * lax.axis_size("gy") * z_count * x_count)
    weight_grad = lax.psum(local_grad, "gy") * norm_factor
    return (input_grad, weight_grad)


def solution(mesh):
    placed = (P(None, "gy", "grp", None), P("ch", "gy", "grp", None), P(None, None, "ch"))
    return jax.shard_map(
        local,
        mesh=mesh,
        in_specs=placed,
        out_specs=(P("ch", "gy", "grp", None), P("grp", None, "ch")),
        check_vma=False,
    )
```

profile of v0, /device:TPU:0, one launch (start us, length us, event | category | flops | bytes accessed | tf_op | source)
XLA Modules:
  0.0 311.7 jit_solution(372415313402467962)
XLA Ops:
  8.1 2.3 copy.71
  10.3 1.3 collective-permute-start.1
  11.6 6.3 %collective-permute-start = (bf16[128,1,8,256]{0,3,2,1:T(8,128)(2,1)}, bf16[128,1,8,256]{0,3,2,1:T(8,128)(2,1)}, u32[]{:S(2)}, u32[]{:S(2)}) collective-permute-start(bf16[128,1,8,256]{0,3,2,1:T(8,128)(2,1)} %copy.71), channel_id=1, source_target_pairs={{0,2},{2,4},{4,6},{6,8},{8,10},{10,12},{12,14},{1,3},{3,5},{5,7},{... | collective-permute-start | bytes 1572872 | tf_op jit(solution)/shard_map/ppermute | solution.py:13
  17.9 1.6 copy.80
  19.6 1.3 collective-permute-start.3
  20.9 5.6 %collective-permute-start.2 = (bf16[256,1,8,256]{0,3,2,1:T(8,128)(2,1)S(1)}, bf16[256,1,8,256]{0,3,2,1:T(8,128)(2,1)}, u32[]{:S(2)}, u32[]{:S(2)}) collective-permute-start(bf16[256,1,8,256]{0,3,2,1:T(8,128)(2,1)S(1)} %copy.80), channel_id=1, source_target_pairs={{0,2},{2,4},{4,6},{6,8},{8,10},{10,12},{12,14},{1,3},{3,5},{5,7},{... | collective-permute-start | bytes 3145736 | tf_op jit(solution)/shard_map/ppermute | solution.py:13
  26.5 2.6 copy.75
  30.1 1.2 fusion.160
  31.4 30.0 %collective-permute-done = bf16[128,1,8,256]{0,3,2,1:T(8,128)(2,1)} collective-permute-done((bf16[128,1,8,256]{0,3,2,1:T(8,128)(2,1)}, bf16[128,1,8,256]{0,3,2,1:T(8,128)(2,1)}, u32[]{:S(2)}, u32[]{:S(2)}) %collective-permute-start) | collective-permute-done | bytes 524320 | tf_op jit(solution)/shard_map/ppermute | solution.py:13
  61.4 1.5 pad_maximum_fusion.1
  62.9 1.3 fusion.161
  64.2 1.2 fusion.162
  65.4 1.2 fusion.163
  66.6 1.6 fusion.164
  72.8 2.7 copy-done.4
  75.5 8.2 %collective-permute-done.2 = bf16[256,1,8,256]{0,3,2,1:T(8,128)(2,1)} collective-permute-done((bf16[256,1,8,256]{0,3,2,1:T(8,128)(2,1)S(1)}, bf16[256,1,8,256]{0,3,2,1:T(8,128)(2,1)}, u32[]{:S(2)}, u32[]{:S(2)}) %collective-permute-start.2) | collective-permute-done | bytes 1048608 | tf_op jit(solution)/shard_map/ppermute | solution.py:13
  83.7 1.9 pad_maximum_fusion
  85.5 2.6 fusion.156
  88.1 2.5 fusion.157
  90.6 2.7 fusion.158
  93.4 3.0 fusion.159
  96.4 2.2 copy.112
  98.6 3.0 fusion.27
  101.6 2.4 fusion.26
  104.0 1.5 fusion.25
  105.5 1.5 fusion.24
  107.0 1.1 fusion.23
  108.2 2.2 copy.113
  110.4 2.2 copy.114
  112.6 3.0 fusion.22
  115.6 3.0 fusion.21
  118.6 1.1 fusion.20
  119.7 1.5 fusion.19
  121.2 1.5 fusion.18
  123.8 1.5 fusion.16
  125.3 1.5 fusion.15
  126.8 1.1 fusion.14
  128.0 2.2 copy.115
  130.2 2.2 copy.116
  132.4 3.0 fusion.13
  135.4 3.0 fusion.12
  138.4 1.1 fusion.11
  139.5 1.5 fusion.10
  141.0 1.5 fusion.9
  143.6 1.5 fusion.7
  145.1 1.5 fusion.6
  146.6 1.1 fusion.5
  147.8 1.8 copy.117
  149.6 2.9 fusion.4
  152.5 1.6 fusion.3
  155.2 1.5 fusion.1
  157.6 2.7 bitcast_dynamic-update-slice_fusion
  160.3 1.6 bitcast_dynamic-update-slice_fusion.10
  163.6 1.6 bitcast_dynamic-update-slice_fusion.8
  165.2 6.6 %copy.74 = bf16[9,128,1,2048]{3,1,0,2:T(8,128)(2,1)} copy(bf16[9,128,1,2048]{1,3,2,0:T(8,128)(2,1)} %get-tuple-element.73) | data formatting | bytes 9437184 | tf_op jit(solution)/shard_map/stack | solution.py:47
  171.8 6.7 %copy.76 = bf16[9,128,1,2048]{3,1,0,2:T(8,128)(2,1)} copy(bf16[9,128,1,2048]{1,3,2,0:T(8,128)(2,1)} %get-tuple-element.72) | data formatting | bytes 9437184 | tf_op jit(solution)/shard_map/stack | solution.py:47
  178.5 6.9 %copy.79 = bf16[9,128,1,2048]{3,1,0,2:T(8,128)(2,1)} copy(bf16[9,128,1,2048]{1,3,2,0:T(8,128)(2,1)} %get-tuple-element.62) | data formatting | bytes 9437184 | tf_op jit(solution)/shard_map/stack | solution.py:47
  185.4 4.2 %fusion.165 = f32[2048,256]{1,0:T(8,128)S(1)} fusion(bf16[1152,2048]{1,0:T(8,128)(2,1)} %bitcast.359, bf16[256,1152]{0,1:T(8,128)(2,1)S(1)} %bitcast.367), kind=kOutput, calls=%fused_computation.235 | convolution fusion | flops 1207959552 | bytes 7405568 | tf_op jit(solution)/shard_map/dot_general | solution.py:68
  189.6 1.7 convolution_add_fusion.1
  192.2 3.0 fusion
  195.3 102.3 %all-reduce.50.cloned.1.call-done = f32[27,256,128]{2,1,0:T(8,128)} async-done(((f32[27,256,128]{2,1,0:T(8,128)}), f32[27,256,128]{2,1,0:T(8,128)}) %all-reduce.50.cloned.1.call-update) | async-done | bytes 3538960 | tf_op jit(solution)/shard_map/psum | solution.py:94
  297.6 4.2 %broadcast_multiply_fusion = f32[27,256,128]{2,1,0:T(8,128)} fusion(f32[27,256,128]{2,1,0:T(8,128)} %all-reduce.50.cloned.1.call-done), kind=kLoop, calls=%fused_computation.4 | loop fusion | flops 884736 | bytes 7077888 | tf_op jit(solution)/shard_map/mul | solution.py:94
  301.7 1.3 convert_element_type.3
  303.0 1.2 copy.110
  (108 shorter events, 12.4 us)
Async XLA Ops:
  8.0 21.2 %copy-start.14 = (bf16[128,1,8,256]{3,2,1,0:T(8,128)(2,1)S(1)}, bf16[128,1,8,256]{3,2,1,0:T(8,128)(2,1)}, u32[]{:S(2)}) copy-start(bf16[128,1,8,256]{3,2,1,0:T(8,128)(2,1)} %param.4) | copy-start | bytes 1572868
  8.0 289.6 %all-reduce.50.cloned.1.call-start = ((), (), s32[]{:S(2)}) async-start(), calls=%async_computation.2 | async-start | bytes 7077888 | tf_op jit(solution)/shard_map/psum | solution.py:94
  10.3 21.0 %collective-permute-start.1 = (bf16[128,1,8,256]{0,3,2,1:T(8,128)(2,1)}, bf16[128,1,8,256]{0,3,2,1:T(8,128)(2,1)}, u32[]{:S(2)}, u32[]{:S(2)}) collective-permute-start(bf16[128,1,8,256]{0,3,2,1:T(8,128)(2,1)} %copy.71), channel_id=1, source_target_pairs={{2,0},{4,2},{6,4},{8,6},{10,8},{12,10},{14,12},{3,1},{5,3},{7,5},{... | collective-permute-start | bytes 1572872 | tf_op jit(solution)/shard_map/ppermute | solution.py:16
  11.6 49.8 %collective-permute-start = (bf16[128,1,8,256]{0,3,2,1:T(8,128)(2,1)}, bf16[128,1,8,256]{0,3,2,1:T(8,128)(2,1)}, u32[]{:S(2)}, u32[]{:S(2)}) collective-permute-start(bf16[128,1,8,256]{0,3,2,1:T(8,128)(2,1)} %copy.71), channel_id=1, source_target_pairs={{0,2},{2,4},{4,6},{6,8},{8,10},{10,12},{12,14},{1,3},{3,5},{5,7},{... | collective-permute-start | bytes 1572872 | tf_op jit(solution)/shard_map/ppermute | solution.py:13
  19.6 11.8 %copy-start.8 = (bf16[256,1,8,256]{0,3,2,1:T(8,128)(2,1)}, bf16[256,1,8,256]{0,3,2,1:T(8,128)(2,1)S(1)}, u32[]{:S(2)}) copy-start(bf16[256,1,8,256]{0,3,2,1:T(8,128)(2,1)S(1)} %copy.80) | copy-start | bytes 3145732
  19.6 53.2 %collective-permute-start.3 = (bf16[256,1,8,256]{0,3,2,1:T(8,128)(2,1)S(1)}, bf16[256,1,8,256]{0,3,2,1:T(8,128)(2,1)}, u32[]{:S(2)}, u32[]{:S(2)}) collective-permute-start(bf16[256,1,8,256]{0,3,2,1:T(8,128)(2,1)S(1)} %copy.80), channel_id=1, source_target_pairs={{2,0},{4,2},{6,4},{8,6},{10,8},{12,10},{14,12},{3,1},{5,3},{7,5},{... | collective-permute-start | bytes 3145736 | tf_op jit(solution)/shard_map/ppermute | solution.py:16
  20.9 62.8 %collective-permute-start.2 = (bf16[256,1,8,256]{0,3,2,1:T(8,128)(2,1)S(1)}, bf16[256,1,8,256]{0,3,2,1:T(8,128)(2,1)}, u32[]{:S(2)}, u32[]{:S(2)}) collective-permute-start(bf16[256,1,8,256]{0,3,2,1:T(8,128)(2,1)S(1)} %copy.80), channel_id=1, source_target_pairs={{0,2},{2,4},{4,6},{6,8},{8,10},{10,12},{12,14},{1,3},{3,5},{5,7},{... | collective-permute-start | bytes 3145736 | tf_op jit(solution)/shard_map/ppermute | solution.py:13
  70.8 12.8 %copy-start.9 = (bf16[256,1,8,256]{0,3,2,1:T(8,128)(2,1)S(1)}, bf16[256,1,8,256]{0,3,2,1:T(8,128)(2,1)}, u32[]{:S(2)}) copy-start(bf16[256,1,8,256]{0,3,2,1:T(8,128)(2,1)} %copy-done.8) | copy-start | bytes 3145732
  71.9 3.6 %copy-start.4 = (bf16[9,128,1,2048]{1,3,2,0:T(8,128)(2,1)}, bf16[9,128,1,2048]{1,3,2,0:T(8,128)(2,1)S(1)}, u32[]{:S(2)}) copy-start(bf16[9,128,1,2048]{1,3,2,0:T(8,128)(2,1)S(1)} %get-tuple-element.60) | copy-start | bytes 14155780
  71.9 11.8 %copy-start.6 = (bf16[9,128,1,2048]{1,3,2,0:T(8,128)(2,1)}, bf16[9,128,1,2048]{1,3,2,0:T(8,128)(2,1)S(1)}, u32[]{:S(2)}) copy-start(bf16[9,128,1,2048]{1,3,2,0:T(8,128)(2,1)S(1)} %get-tuple-element.61) | copy-start | bytes 14155780
  72.8 2.7 copy-start.5
  98.6 5.4 %copy-start = (bf16[16,8,8,256]{3,1,2,0:T(8,128)(2,1)S(1)}, bf16[16,8,8,256]{3,1,2,0:T(8,128)(2,1)}, u32[]{:S(2)}) copy-start(bf16[16,8,8,256]{3,1,2,0:T(8,128)(2,1)} %copy.118) | copy-start | bytes 1572868
  98.6 5.4 %copy-start.30 = (bf16[256,1,1793]{0,2,1:T(8,128)(2,1)S(1)}, bf16[256,1,1793]{0,2,1:T(8,128)(2,1)}, u32[]{:S(2)}) copy-start(bf16[256,1,1793]{0,2,1:T(8,128)(2,1)} %get-tuple-element.25) | copy-start | bytes 2754052
  98.6 6.9 %copy-start.26 = (bf16[256,1,2047]{0,2,1:T(8,128)(2,1)S(1)}, bf16[256,1,2047]{0,2,1:T(8,128)(2,1)}, u32[]{:S(2)}) copy-start(bf16[256,1,2047]{0,2,1:T(8,128)(2,1)} %get-tuple-element.31) | copy-start | bytes 3144196
  112.6 6.0 %copy-start.1 = (bf16[16,8,8,256]{3,1,2,0:T(8,128)(2,1)S(1)}, bf16[16,8,8,256]{3,1,2,0:T(8,128)(2,1)}, u32[]{:S(2)}) copy-start(bf16[16,8,8,256]{3,1,2,0:T(8,128)(2,1)} %copy.118) | copy-start | bytes 1572868
  112.6 6.0 %copy-start.12 = (bf16[256,1,1792]{2,0,1:T(8,128)(2,1)S(1)}, bf16[256,1,1792]{2,0,1:T(8,128)(2,1)}, u32[]{:S(2)}) copy-start(bf16[256,1,1792]{2,0,1:T(8,128)(2,1)} %copy.113) | copy-start | bytes 2752516
  112.6 7.1 %copy-start.35 = (bf16[256,1,1791]{0,2,1:T(8,128)(2,1)S(1)}, bf16[256,1,1791]{0,2,1:T(8,128)(2,1)}, u32[]{:S(2)}) copy-start(bf16[256,1,1791]{0,2,1:T(8,128)(2,1)} %get-tuple-element.12) | copy-start | bytes 2750980
  115.6 5.6 %copy-start.34 = (bf16[256,1,1791]{0,2,1:T(8,128)(2,1)S(1)}, bf16[256,1,1791]{0,2,1:T(8,128)(2,1)}, u32[]{:S(2)}) copy-start(bf16[256,1,1791]{0,2,1:T(8,128)(2,1)} %get-tuple-element.11) | copy-start | bytes 2750980
  118.6 4.2 %copy-start.10 = (bf16[256,1,1792]{2,0,1:T(8,128)(2,1)S(1)}, bf16[256,1,1792]{2,0,1:T(8,128)(2,1)}, u32[]{:S(2)}) copy-start(bf16[256,1,1792]{2,0,1:T(8,128)(2,1)} %copy.114) | copy-start | bytes 2752516
  119.7 4.2 %copy-start.29 = (bf16[256,1,1793]{0,2,1:T(8,128)(2,1)S(1)}, bf16[256,1,1793]{0,2,1:T(8,128)(2,1)}, u32[]{:S(2)}) copy-start(bf16[256,1,1793]{0,2,1:T(8,128)(2,1)} %get-tuple-element.23) | copy-start | bytes 2754052
  121.2 4.1 %copy-start.25 = (bf16[256,1,2047]{0,2,1:T(8,128)(2,1)S(1)}, bf16[256,1,2047]{0,2,1:T(8,128)(2,1)}, u32[]{:S(2)}) copy-start(bf16[256,1,2047]{0,2,1:T(8,128)(2,1)} %get-tuple-element.29) | copy-start | bytes 3144196
  132.4 6.0 %copy-start.2 = (bf16[16,8,8,256]{3,1,2,0:T(8,128)(2,1)S(1)}, bf16[16,8,8,256]{3,1,2,0:T(8,128)(2,1)}, u32[]{:S(2)}) copy-start(bf16[16,8,8,256]{3,1,2,0:T(8,128)(2,1)} %copy.118) | copy-start | bytes 1572868
  132.4 6.0 %copy-start.13 = (bf16[256,1,1792]{2,0,1:T(8,128)(2,1)S(1)}, bf16[256,1,1792]{2,0,1:T(8,128)(2,1)}, u32[]{:S(2)}) copy-start(bf16[256,1,1792]{2,0,1:T(8,128)(2,1)} %copy.115) | copy-start | bytes 2752516
  132.4 7.1 %copy-start.33 = (bf16[256,1,1791]{0,2,1:T(8,128)(2,1)S(1)}, bf16[256,1,1791]{0,2,1:T(8,128)(2,1)}, u32[]{:S(2)}) copy-start(bf16[256,1,1791]{0,2,1:T(8,128)(2,1)} %get-tuple-element.10) | copy-start | bytes 2750980
  135.4 5.6 %copy-start.32 = (bf16[256,1,1791]{0,2,1:T(8,128)(2,1)S(1)}, bf16[256,1,1791]{0,2,1:T(8,128)(2,1)}, u32[]{:S(2)}) copy-start(bf16[256,1,1791]{0,2,1:T(8,128)(2,1)} %get-tuple-element.9) | copy-start | bytes 2750980
  138.4 4.2 %copy-start.11 = (bf16[256,1,1792]{2,0,1:T(8,128)(2,1)S(1)}, bf16[256,1,1792]{2,0,1:T(8,128)(2,1)}, u32[]{:S(2)}) copy-start(bf16[256,1,1792]{2,0,1:T(8,128)(2,1)} %copy.116) | copy-start | bytes 2752516
  139.5 4.2 %copy-start.28 = (bf16[256,1,1793]{0,2,1:T(8,128)(2,1)S(1)}, bf16[256,1,1793]{0,2,1:T(8,128)(2,1)}, u32[]{:S(2)}) copy-start(bf16[256,1,1793]{0,2,1:T(8,128)(2,1)} %get-tuple-element.21) | copy-start | bytes 2754052
  141.0 4.1 %copy-start.24 = (bf16[256,1,2047]{0,2,1:T(8,128)(2,1)S(1)}, bf16[256,1,2047]{0,2,1:T(8,128)(2,1)}, u32[]{:S(2)}) copy-start(bf16[256,1,2047]{0,2,1:T(8,128)(2,1)} %get-tuple-element.27) | copy-start | bytes 3144196
  147.8 4.7 %copy-start.3 = (bf16[16,8,8,256]{3,1,2,0:T(8,128)(2,1)S(1)}, bf16[16,8,8,256]{3,1,2,0:T(8,128)(2,1)}, u32[]{:S(2)}) copy-start(bf16[16,8,8,256]{3,1,2,0:T(8,128)(2,1)} %copy.118) | copy-start | bytes 1572868
  147.8 4.7 %copy-start.27 = (bf16[256,1,1793]{0,2,1:T(8,128)(2,1)S(1)}, bf16[256,1,1793]{0,2,1:T(8,128)(2,1)}, u32[]{:S(2)}) copy-start(bf16[256,1,1793]{0,2,1:T(8,128)(2,1)} %get-tuple-element.20) | copy-start | bytes 2754052
  149.6 5.6 %copy-start.31 = (bf16[256,1,1791]{0,2,1:T(8,128)(2,1)S(1)}, bf16[256,1,1791]{0,2,1:T(8,128)(2,1)}, u32[]{:S(2)}) copy-start(bf16[256,1,1791]{0,2,1:T(8,128)(2,1)} %get-tuple-element.8) | copy-start | bytes 2750980
  154.1 2.7 copy-start.23
  155.2 2.4 copy-start.15
  155.2 2.4 copy-start.16
  156.6 3.7 %copy-start.17 = (bf16[128,1,1793]{0,2,1:T(8,128)(2,1)S(1)}, bf16[128,1,1793]{0,2,1:T(8,128)(2,1)}, u32[]{:S(2)}) copy-start(bf16[128,1,1793]{0,2,1:T(8,128)(2,1)} %get-tuple-element.49) | copy-start | bytes 1377028
  156.6 3.7 %copy-start.18 = (bf16[128,1,1793]{0,2,1:T(8,128)(2,1)S(1)}, bf16[128,1,1793]{0,2,1:T(8,128)(2,1)}, u32[]{:S(2)}) copy-start(bf16[128,1,1793]{0,2,1:T(8,128)(2,1)} %get-tuple-element.51) | copy-start | bytes 1377028
  156.7 5.2 %copy-start.22 = (bf16[128,1,1792]{0,2,1:T(8,128)(2,1)S(1)}, bf16[128,1,1792]{0,2,1:T(8,128)(2,1)}, u32[]{:S(2)}) copy-start(bf16[128,1,1792]{0,2,1:T(8,128)(2,1)} %get-tuple-element.43) | copy-start | bytes 1376260
  156.7 6.1 %copy-start.21 = (bf16[128,1,1792]{0,2,1:T(8,128)(2,1)S(1)}, bf16[128,1,1792]{0,2,1:T(8,128)(2,1)}, u32[]{:S(2)}) copy-start(bf16[128,1,1792]{0,2,1:T(8,128)(2,1)} %get-tuple-element.45) | copy-start | bytes 1376260
  156.7 145.1 %reduce-scatter.2.cloned.1.call-start = ((), (), s32[]{:S(2)}) async-start(), calls=%async_computation.1 | async-start | bytes 3145728 | tf_op jit(solution)/shard_map/reduce_scatter | solution.py:71
  157.6 6.0 %copy-start.19 = (bf16[128,1,1791]{0,2,1:T(8,128)(2,1)S(1)}, bf16[128,1,1791]{0,2,1:T(8,128)(2,1)}, u32[]{:S(2)}) copy-start(bf16[128,1,1791]{0,2,1:T(8,128)(2,1)} %get-tuple-element.37) | copy-start | bytes 1375492
  157.6 6.0 %copy-start.20 = (bf16[128,1,1791]{0,2,1:T(8,128)(2,1)S(1)}, bf16[128,1,1791]{0,2,1:T(8,128)(2,1)}, u32[]{:S(2)}) copy-start(bf16[128,1,1791]{0,2,1:T(8,128)(2,1)} %get-tuple-element.39) | copy-start | bytes 1375492
  178.5 6.9 %copy-start.38 = (bf16[256,9,128]{0,2,1:T(8,128)(2,1)S(1)}, bf16[256,9,128]{0,2,1:T(8,128)(2,1)}, u32[]{:S(2)}) copy-start(bf16[256,9,128]{0,2,1:T(8,128)(2,1)} %get-tuple-element.34) | copy-start | bytes 1769476
  178.5 11.1 %slice-start = ((s8[4718592]{0:T(1024)(128)(4,1)}), s8[524288]{0:T(1024)(128)(4,1)S(1)}, s32[]{:S(2)}) async-start(s8[4718592]{0:T(1024)(128)(4,1)} %bitcast.360), calls=%async_computation.3 | async-start | bytes 1048576
  185.4 4.2 %slice-start.1 = ((s8[4718592]{0:T(1024)(128)(4,1)}), s8[4194304]{0:T(1024)(128)(4,1)S(1)}, s32[]{:S(2)}) async-start(s8[4718592]{0:T(1024)(128)(4,1)} %bitcast.360), calls=%async_computation.4 | async-start | bytes 8388608
  185.4 4.2 %copy-start.37 = (bf16[256,9,128]{0,2,1:T(8,128)(2,1)S(1)}, bf16[256,9,128]{0,2,1:T(8,128)(2,1)}, u32[]{:S(2)}) copy-start(bf16[256,9,128]{0,2,1:T(8,128)(2,1)} %get-tuple-element.33) | copy-start | bytes 1769476
  189.6 2.4 copy-start.7
  189.6 2.6 copy-start.36
Sparse Core Ops, SparseCore 0:
  156.8 140.7 all-reduce.49
Sparse Core Ops, SparseCore 1:
  195.3 10.7 reduce-scatter.1
where the time goes:
time: 313 us; the launch traced here: 312 us
  waiting for transfers between devices  141 us (45%)
  local copies, waits for them, and re-layouts  65.7 us (21%)
  matrix products  56.2 us (18%)
  other arithmetic  18.9 us (6%)
  between operations  15.8 us (5%)
  starting transfers between devices  14.6 us (5%)
    psum x1, waiting for transfers between devices, local(): weight_grad = lax.psum(local_grad, 'gy') * norm_factor  102 us
    dot_general x27, matrix products, local(): lax.dot_general(moved, grad_flat, (((1,), (1,)), ((), ())), preferred_ele...  47.3 us
    ppermute x2, waiting for transfers between devices, padded(): lax.ppermute(lax.slice_in_dim(block, block.shape[dim] - width, None, axis...  38.2 us
    unnamed x99, local copies, waits for them, and re-layouts  28.2 us
    another operation x3, local copies, waits for them, and re-layouts, grad_group(): stacked = jnp.stack(pieces_list, 0)  20.2 us
    ppermute x2, starting transfers between devices, padded(): lax.ppermute(lax.slice_in_dim(block, block.shape[dim] - width, None, axis...  12 us
    slice x4, local copies, waits for them, and re-layouts, shift_cells(): moved = jnp.concatenate([flat[..., -offset:], filler], axis=-1)  10.8 us
    dot_general x3, matrix products, local(): jnp.dot(tap_cols, stacks[partial_y_off], preferred_element_type=jnp.float32)  8.93 us
  transfers between devices with their start and end apart: 6, of which 3 were waited for; matrix products, arithmetic and copies ran while one was open for 19% of the time, Pallas kernels for 0%

commit v1 on v0

--- a/solution.py
+++ b/solution.py
@@ -91,7 +91,7 @@
                 )
     local_grad = jnp.stack(tap_grads, 0)
     norm_factor = 1.0 / math.sqrt(row_count * lax.axis_size("gy") * z_count * x_count)
-    weight_grad = lax.psum(local_grad, "gy") * norm_factor
+    weight_grad = jnp.sum(lax.all_gather(local_grad, "gy"), axis=0) * norm_factor
     return (input_grad, weight_grad)
 
 

time: 313 us -> 749 us (2.39)
  waiting for transfers between devices: 141 us -> 569 us
  other arithmetic: 18.9 us -> 32.6 us
    all_gather x0 -> x1, waiting for transfers between devices: none -> 538 us  [local(): lax.all_gather(local_grad, 'gy')]
    psum x1 -> x0, waiting for transfers between devices: 102 us -> none  [local(): weight_grad = lax.psum(local_grad, 'gy') * norm_factor]
    reduce_sum x0 -> x1, other arithmetic: none -> 11.8 us  [local(): jnp.sum(lax.all_gather(local_grad, 'gy'), axis=0) * norm_factor]
    ppermute x2, waiting for transfers between devices: 38.2 us -> 30.1 us  [padded(): lax.ppermute(lax.slice_in_dim(block, block.shape[dim] - width, None, axis...]
    unnamed x99 -> x73, local copies, waits for them, and re-layouts: 28.2 us -> 28.3 us
  transfers between devices with their start and end apart: 6 -> 6, of which waited for: 3 -> 2; matrix products, arithmetic and copies ran while one was open for 19% -> 18% of each run, Pallas kernels for 0% -> 0%
where the time goes in v1:
time: 749 us; the launch traced here: 748 us
  waiting for transfers between devices  569 us (76%)
  local copies, waits for them, and re-layouts  62.1 us (8%)
  matrix products  54.6 us (7%)
  other arithmetic  32.6 us (4%)
  between operations  15.7 us (2%)
  starting transfers between devices  14.6 us (2%)
    all_gather x1, waiting for transfers between devices, local(): lax.all_gather(local_grad, 'gy')  538 us
    dot_general x27, matrix products, local(): lax.dot_general(moved, grad_flat, (((1,), (1,)), ((), ())), preferred_ele...  45.7 us
    ppermute x2, waiting for transfers between devices, padded(): lax.ppermute(lax.slice_in_dim(block, block.shape[dim] - width, None, axis...  30.1 us
    unnamed x73, local copies, waits for them, and re-layouts  28.3 us
    another operation x3, local copies, waits for them, and re-layouts, grad_group(): stacked = jnp.stack(pieces_list, 0)  20.3 us
  transfers between devices with their start and end apart: 6, of which 2 were waited for; matrix products, arithmetic and copies ran while one was open for 18% of the time, Pallas kernels for 0%

profile of v1, /device:TPU:0, one launch (start us, length us, event | category | flops | bytes accessed | tf_op | source)
XLA Modules:
  0.0 748.3 jit_solution(11213918341136960621)
XLA Ops:
  8.1 2.3 copy.111
  10.3 1.3 collective-permute-start.1
  11.6 6.3 collective-permute-start
  17.9 1.6 copy.120
  19.6 1.3 collective-permute-start.3
  20.9 5.7 collective-permute-start.2
  26.5 2.6 copy.115
  30.1 1.2 fusion.160
  31.3 30.1 %collective-permute-done = bf16[128,1,8,256]{0,3,2,1:T(8,128)(2,1)} collective-permute-done((bf16[128,1,8,256]{0,3,2,1:T(8,128)(2,1)}, bf16[128,1,8,256]{0,3,2,1:T(8,128)(2,1)}, u32[]{:S(2)}, u32[]{:S(2)}) %collective-permute-start) | collective-permute-done | bytes 524320 | tf_op jit(solution)/shard_map/ppermute | solution.py:13
  61.4 1.5 pad_maximum_fusion.1
  64.6 1.4 bitcast_dynamic-update-slice_fusion.7
  67.1 1.4 bitcast_dynamic-update-slice_fusion.5
  68.4 1.6 bitcast_dynamic-update-slice_fusion.4
  72.0 1.1 bitcast_dynamic-update-slice_fusion.12
  73.1 1.2 fusion.100
  74.3 1.1 bitcast_dynamic-update-slice_fusion.3
  77.4 1.8 bitcast_dynamic-update-slice_fusion
  79.2 1.5 bitcast_dynamic-update-slice_fusion.10
  82.5 1.5 bitcast_dynamic-update-slice_fusion.8
  84.0 6.7 copy.114
  90.7 6.7 copy.116
  97.4 6.9 copy.119
  104.3 4.1 fusion.165
  108.5 1.7 convolution_add_fusion.1
  110.8 3.1 fusion
  114.0 2.2 pad_maximum_fusion
  116.2 2.6 fusion.156
  118.8 2.5 fusion.157
  121.3 2.6 fusion.158
  124.0 2.9 fusion.159
  126.8 2.2 copy.152
  129.1 3.0 fusion.27
  132.1 2.4 fusion.26
  134.5 1.5 fusion.25
  136.0 1.5 fusion.24
  137.5 1.1 fusion.23
  138.6 2.2 copy.153
  140.8 3.0 fusion.22
  143.9 3.0 fusion.21
  147.9 1.5 fusion.19
  149.4 1.5 fusion.18
  150.9 2.2 copy.154
  153.2 2.2 copy.155
  155.4 2.2 copy.156
  157.6 2.2 copy.157
  159.8 2.5 fusion.17
  162.3 2.9 fusion.16
  165.2 1.5 fusion.15
  166.8 1.1 fusion.14
  167.9 1.5 fusion.13
  169.4 1.5 fusion.12
  172.1 1.5 fusion.10
  173.6 1.5 fusion.9
  176.2 1.5 fusion.7
  177.7 1.5 fusion.6
  179.2 1.1 fusion.5
  180.4 1.5 fusion.4
  181.9 1.6 fusion.3
  184.5 1.5 fusion.1
  186.0 1.3 convert_element_type.3
  187.3 1.2 copy.150
  188.5 538.4 %all-gather.3.cloned.1.call-done = f32[216,256,128]{2,1,0:T(8,128)} async-done(((f32[27,256,128]{2,1,0:T(8,128)}), f32[216,256,128]{2,1,0:T(8,128)}) %all-gather.3.cloned.1.call-update) | async-done | bytes 28311568 | tf_op jit(solution)/shard_map/all_gather | solution.py:94
  727.0 11.8 %reduce_sum.9 = f32[27,256,128]{2,1,0:T(8,128)S(1)} reduce(f32[8,27,256,128]{3,2,1,0:T(8,128)} %bitcast.331, f32[]{:T(128)} %constant.141.clone.1), dimensions={0}, to_apply=%region_1.2 | reduce | flops 6193152 | bytes 31850500 | tf_op jit(solution)/shard_map/reduce_sum | solution.py:94
  738.8 2.0 broadcast_multiply_fusion
  (83 shorter events, 14.5 us)
Async XLA Ops:
  8.0 21.2 %copy-start.9 = (bf16[128,1,8,256]{3,2,1,0:T(8,128)(2,1)S(1)}, bf16[128,1,8,256]{3,2,1,0:T(8,128)(2,1)}, u32[]{:S(2)}) copy-start(bf16[128,1,8,256]{3,2,1,0:T(8,128)(2,1)} %param.4) | copy-start | bytes 1572868
  8.0 178.0 %reduce-scatter.2.cloned.1.call-start = ((), (), s32[]{:S(2)}) async-start(), calls=%async_computation.1 | async-start | bytes 3145728 | tf_op jit(solution)/shard_map/reduce_scatter | solution.py:71
  10.3 21.0 %collective-permute-start.1 = (bf16[128,1,8,256]{0,3,2,1:T(8,128)(2,1)}, bf16[128,1,8,256]{0,3,2,1:T(8,128)(2,1)}, u32[]{:S(2)}, u32[]{:S(2)}) collective-permute-start(bf16[128,1,8,256]{0,3,2,1:T(8,128)(2,1)} %copy.111), channel_id=1, source_target_pairs={{2,0},{4,2},{6,4},{8,6},{10,8},{12,10},{14,12},{3,1},{5,3},{7,5},{... | collective-permute-start | bytes 1572872 | tf_op jit(solution)/shard_map/ppermute | solution.py:16
  11.6 49.8 %collective-permute-start = (bf16[128,1,8,256]{0,3,2,1:T(8,128)(2,1)}, bf16[128,1,8,256]{0,3,2,1:T(8,128)(2,1)}, u32[]{:S(2)}, u32[]{:S(2)}) collective-permute-start(bf16[128,1,8,256]{0,3,2,1:T(8,128)(2,1)} %copy.111), channel_id=1, source_target_pairs={{0,2},{2,4},{4,6},{6,8},{8,10},{10,12},{12,14},{1,3},{3,5},{5,7},{... | collective-permute-start | bytes 1572872 | tf_op jit(solution)/shard_map/ppermute | solution.py:13
  19.6 11.7 %copy-start.4 = (bf16[256,1,8,256]{0,3,2,1:T(8,128)(2,1)}, bf16[256,1,8,256]{0,3,2,1:T(8,128)(2,1)S(1)}, u32[]{:S(2)}) copy-start(bf16[256,1,8,256]{0,3,2,1:T(8,128)(2,1)S(1)} %copy.120) | copy-start | bytes 3145732
  19.6 94.4 %collective-permute-start.3 = (bf16[256,1,8,256]{0,3,2,1:T(8,128)(2,1)S(1)}, bf16[256,1,8,256]{0,3,2,1:T(8,128)(2,1)}, u32[]{:S(2)}, u32[]{:S(2)}) collective-permute-start(bf16[256,1,8,256]{0,3,2,1:T(8,128)(2,1)S(1)} %copy.120), channel_id=1, source_target_pairs={{2,0},{4,2},{6,4},{8,6},{10,8},{12,10},{14,12},{3,1},{5,3},{7,5},{... | collective-permute-start | bytes 3145736 | tf_op jit(solution)/shard_map/ppermute | solution.py:16
  20.9 93.1 %collective-permute-start.2 = (bf16[256,1,8,256]{0,3,2,1:T(8,128)(2,1)S(1)}, bf16[256,1,8,256]{0,3,2,1:T(8,128)(2,1)}, u32[]{:S(2)}, u32[]{:S(2)}) collective-permute-start(bf16[256,1,8,256]{0,3,2,1:T(8,128)(2,1)S(1)} %copy.120), channel_id=1, source_target_pairs={{0,2},{2,4},{4,6},{6,8},{8,10},{10,12},{12,14},{1,3},{3,5},{5,7},{... | collective-permute-start | bytes 3145736 | tf_op jit(solution)/shard_map/ppermute | solution.py:13
  97.4 6.9 copy-start.25
  97.4 11.0 %slice-start = ((s8[4718592]{0:T(1024)(128)(4,1)}), s8[524288]{0:T(1024)(128)(4,1)S(1)}, s32[]{:S(2)}) async-start(s8[4718592]{0:T(1024)(128)(4,1)} %bitcast.362), calls=%async_computation.3 | async-start | bytes 1048576
  104.3 4.1 slice-start.1
  104.3 4.1 copy-start.24
  108.5 2.3 copy-start.3
  113.9 613.1 %all-gather.3.cloned.1.call-start = ((), (), s32[]{:S(2)}) async-start(), calls=%async_computation.2 | async-start | bytes 31850496 | tf_op jit(solution)/shard_map/all_gather | solution.py:94
  129.1 5.4 copy-start
  129.1 5.4 copy-start.18
  129.1 6.9 copy-start.14
  140.8 6.0 copy-start.1
  140.8 6.0 copy-start.8
  140.8 7.1 copy-start.23
  143.9 5.5 copy-start.22
  159.8 5.4 copy-start.2
  159.8 5.4 copy-start.13
  162.3 5.6 copy-start.12
  165.2 4.2 copy-start.17
  166.8 4.2 copy-start.7
  167.9 4.2 copy-start.21
  169.4 4.2 copy-start.20
  171.0 4.1 copy-start.6
  172.1 4.2 copy-start.16
  173.6 4.1 copy-start.11
  176.2 4.2 copy-start.10
  177.7 4.2 copy-start.15
  179.2 4.2 copy-start.5
  180.4 4.2 copy-start.19
Sparse Core Ops, SparseCore 0:
  114.0 11.0 reduce-scatter.1
Sparse Core Ops, SparseCore 1:
  186.1 540.8 all-gather.2
